TPU v7x, 32 devices: a whole 2x2x4 slice. The times are simulated.
32 devices in a mesh: dp: 4 (over z), expert: 2 (over x), head: 4 (over y, core).
Axes of the slice: x: 2, y: 2, z: 4, core: 2. Of those that a mesh axis runs over, the one named last changes fastest.
Arguments:
- hidden_in: bfloat16 [1024, 7168], P(('dp', 'expert'), 'head'), may hold values from -6 to 6
- grad_out: bfloat16 [1024, 7168], P(('dp', 'expert'), 'head'), may hold values from -6 to 6
- expert_ids: int32 [1024, 8], P(('dp', 'expert')), may hold values from 0 to 255, all different within a row; in each aligned block of 128 rows (0 to 127, 128 to 255, ...) at most 8 rows name the same one
- gate_weights: float32 [1024, 8], P(('dp', 'expert')), may hold values from 0.1 to 1
- w_gate: bfloat16 [8, 7168, 2048], P(('dp', 'expert'), None, 'head'), may hold values from -0.0625 to 0.0625
- w_up: bfloat16 [8, 7168, 2048], P(('dp', 'expert'), None, 'head'), may hold values from -0.0625 to 0.0625
- w_down: bfloat16 [8, 2048, 7168], P(('dp', 'expert'), 'head'), may hold values from -0.125 to 0.125
- latent_kv: bfloat16 [1024, 576], P(('dp', 'expert')), may hold values from -16 to 16
- query: bfloat16 [1024, 12288], P('dp', ('expert', 'head')), may hold values from -240 to 240
- d_attn: bfloat16 [1024, 8192], P('dp', ('expert', 'head')), may hold values from -6 to 6
- w_uk: bfloat16 [512, 8192], P(None, ('expert', 'head')), may hold values from -0.25 to 0.25
- w_uv: bfloat16 [512, 8192], P(None, ('expert', 'head')), may hold values from -0.25 to 0.25
- doc_ids: int32 [1024], P('dp'), may hold values from 0 to 15, never falling along the last dimension, each value on 1 to 256 neighbouring positions
Outputs:
- d_hidden: bfloat16 [1024, 7168], P(('dp', 'expert'), 'head')
- d_gates: bfloat16 [1024, 8], P(('dp', 'expert'))
- d_query: bfloat16 [1024, 12288], P('dp', ('expert', 'head'))
- d_latent_kv: bfloat16 [1024, 576], P(('dp', 'expert'), 'head')
Inputs may be any that keep to these rules, and one draw needn't show every extreme that they name: `expert_ids`: each row names 8 different experts; in each aligned block of 128 rows (the rows of one device) no expert is named by more than 8 rows, a bound that some block reaches. `doc_ids`: document numbers never fall; each document has 1 to 256 tokens.
All inputs are finite; a program needn't handle non-finite values.
Results may differ from a plain program's by a relative error of at most 0.0089.
Values may be sent and summed in bfloat16 or wider, within the bound.
A program may use at most 128 MiB of HBM per device.

v0:
```python
import math
import jax
import jax.numpy as jnp
from jax import lax
from jax.sharding import PartitionSpec as P

TOP = 8
LAT = 512
NOPE = 128
ROPE = 64
VD = 128
CAP = 8
CONTRACT_LAST = (((1,), (1,)), ((), ()))


def expert_backward(rows_x, rows_dy, gate_mat, up_mat, down_mat):
    gate_pre = jnp.dot(rows_x, gate_mat, preferred_element_type=jnp.float32)
    up_pre = jnp.dot(rows_x, up_mat, preferred_element_type=jnp.float32)
    back_hidden = lax.dot_general(
        rows_dy, down_mat, CONTRACT_LAST, preferred_element_type=jnp.float32
    )
    sig_val = jax.nn.sigmoid(gate_pre)
    act_val = gate_pre * sig_val
    gate_part = jnp.sum(act_val * up_pre * back_hidden, axis=1)
    d_up = (back_hidden * act_val).astype(jnp.bfloat16)
    d_pre = (back_hidden * up_pre * sig_val * (1.0 + gate_pre * (1.0 - sig_val))).astype(
        jnp.bfloat16
    )
    row_part = lax.dot_general(
        d_pre, gate_mat, CONTRACT_LAST, preferred_element_type=jnp.float32
    ) + lax.dot_general(d_up, up_mat, CONTRACT_LAST, preferred_element_type=jnp.float32)
    return (row_part, gate_part)


def expert_half(hidden_in, grad_out, expert_ids, gate_weights, w_gate, w_up, w_down):
    window_size = lax.axis_size("dp") * lax.axis_size("expert")
    head_count = lax.axis_size("head")
    tok_local = expert_ids.shape[0]
    route_count = tok_local * TOP
    flat_ids = expert_ids.reshape(route_count)
    inside = flat_ids < window_size
    one_hot = (flat_ids[:, None] == jnp.arange(window_size, dtype=jnp.int32)[None, :]).astype(
        jnp.int32
    )
    earlier = jnp.cumsum(one_hot, axis=0) - one_hot
    slot_num = jnp.sum(earlier * one_hot, axis=1)
    target = jnp.where(inside, flat_ids * CAP + slot_num, window_size * CAP)
    slot_hits = target[None, :] == jnp.arange(window_size * CAP, dtype=jnp.int32)[:, None]
    filled = jnp.any(slot_hits, axis=1)
    route_of_slot = jnp.sum(
        jnp.where(slot_hits, jnp.arange(route_count, dtype=jnp.int32)[None, :], 0), axis=1
    )
    token_of_slot = route_of_slot // TOP
    rows_x, rows_dy = (hidden_in, grad_out)
    send_x = jnp.where(filled[:, None], jnp.take(rows_x, token_of_slot, axis=0), 0)
    send_dy = jnp.where(filled[:, None], jnp.take(rows_dy, token_of_slot, axis=0), 0)
    send_x = send_x.reshape(window_size, CAP, send_x.shape[1])
    send_dy = send_dy.reshape(window_size, CAP, send_dy.shape[1])
    got_x = lax.all_to_all(send_x, ("dp", "expert"), split_axis=0, concat_axis=0, tiled=True)
    got_dy = lax.all_to_all(send_dy, ("dp", "expert"), split_axis=0, concat_axis=0, tiled=True)
    got_x, got_dy = (
        lax.all_gather(got_x, "head", axis=2, tiled=True),
        lax.all_gather(got_dy, "head", axis=2, tiled=True),
    )
    sources = got_x.shape[0]
    items = got_x.shape[1]
    flat_x = got_x.reshape(sources * items, got_x.shape[2])
    flat_dy = got_dy.reshape(sources * items, got_dy.shape[2])
    row_part, gate_part = expert_backward(flat_x, flat_dy, w_gate[0], w_up[0], w_down[0])
    gate_spread = jnp.broadcast_to(gate_part[:, None], (sources * items, head_count))
    summed = lax.psum_scatter(row_part, "head", scatter_dimension=1, tiled=True)
    gate_sum = lax.psum_scatter(gate_spread, "head", scatter_dimension=1, tiled=True)
    back_rows = summed.astype(jnp.bfloat16).reshape(sources, items, summed.shape[1])
    back_gate = gate_sum[:, 0].astype(jnp.bfloat16).reshape(sources, items)
    back_rows, back_gate = (
        lax.all_to_all(back_rows, ("dp", "expert"), split_axis=0, concat_axis=0, tiled=True),
        lax.all_to_all(back_gate, ("dp", "expert"), split_axis=0, concat_axis=0, tiled=True),
    )
    flat_back = back_rows.reshape(window_size * CAP, back_rows.shape[2])
    flat_gate = back_gate.reshape(window_size * CAP)
    safe_target = jnp.where(inside, target, 0)
    route_weight = jnp.where(inside, gate_weights.reshape(route_count), 0.0)
    picked = jnp.take(flat_back, safe_target, axis=0).astype(jnp.float32) * route_weight[:, None]
    d_hidden = jnp.sum(picked.reshape(tok_local, TOP, picked.shape[1]), axis=1).astype(jnp.bfloat16)
    d_gates = jnp.where(inside, jnp.take(flat_gate, safe_target), jnp.zeros((), jnp.bfloat16))
    return (d_hidden, d_gates.reshape(tok_local, TOP))


def attention_half(latent_kv, query, d_attn, w_uk, w_uv, doc_ids):
    seq_len = query.shape[0]
    heads_here = w_uk.shape[1] // NOPE
    score_scale = 1.0 / math.sqrt(NOPE + ROPE)
    w_both = jnp.concatenate([w_uk, w_uv], axis=1)
    piece = lax.all_gather(latent_kv, "expert", axis=0, tiled=True)
    lifted = jnp.dot(piece[:, :LAT], w_both, preferred_element_type=jnp.float32).astype(
        jnp.bfloat16
    )
    keyvals = jnp.concatenate([lifted, piece[:, LAT:]], axis=1)
    key_nope = keyvals[:, : heads_here * NOPE].reshape(seq_len, heads_here, NOPE)
    all_values = keyvals[:, heads_here * NOPE : heads_here * (NOPE + VD)].reshape(
        seq_len, heads_here, VD
    )
    rope_key = keyvals[:, heads_here * (NOPE + VD) :]
    all_keys = jnp.concatenate(
        [key_nope, jnp.broadcast_to(rope_key[:, None, :], (seq_len, heads_here, ROPE))], axis=2
    )
    queries = query.reshape(seq_len, heads_here, NOPE + ROPE)
    douts = d_attn.reshape(seq_len, heads_here, VD)
    positions = jnp.arange(seq_len, dtype=jnp.int32)
    block_rows = min(512, seq_len)
    dkey_sum = jnp.zeros((seq_len, heads_here, NOPE + ROPE), jnp.float32)
    dval_sum = jnp.zeros((seq_len, heads_here, VD), jnp.float32)
    dq_blocks = []
    for block_num in range(seq_len // block_rows):
        first_row = block_num * block_rows
        query_blk = queries[first_row : first_row + block_rows]
        dout_blk = douts[first_row : first_row + block_rows]
        scores = (
            jnp.einsum("qhd,khd->hqk", query_blk, all_keys, preferred_element_type=jnp.float32)
            * score_scale
        )
        allowed = (positions[None, :] <= positions[first_row : first_row + block_rows, None]) & (
            doc_ids[None, :] == doc_ids[first_row : first_row + block_rows, None]
        )
        scores = jnp.where(allowed[None], scores, -1e30)
        top_score = jnp.max(scores, axis=2, keepdims=True)
        expd = jnp.exp(scores - top_score)
        probs = expd / jnp.sum(expd, axis=2, keepdims=True)
        dprobs = jnp.einsum(
            "qhd,khd->hqk", dout_blk, all_values, preferred_element_type=jnp.float32
        )
        inner = jnp.sum(probs * dprobs, axis=2, keepdims=True)
        dscore = (probs * (dprobs - inner) * score_scale).astype(jnp.bfloat16)
        prob_low = probs.astype(jnp.bfloat16)
        dq_blocks.append(
            jnp.einsum("hqk,khd->qhd", dscore, all_keys, preferred_element_type=jnp.float32).astype(
                jnp.bfloat16
            )
        )
        dkey_sum = dkey_sum + jnp.einsum(
            "hqk,qhd->khd", dscore, query_blk, preferred_element_type=jnp.float32
        )
        dval_sum = dval_sum + jnp.einsum(
            "hqk,qhd->khd", prob_low, dout_blk, preferred_element_type=jnp.float32
        )
    d_query = jnp.concatenate(dq_blocks, axis=0).reshape(seq_len, heads_here * (NOPE + ROPE))
    dkey_low = dkey_sum.astype(jnp.bfloat16)
    dval_low = dval_sum.astype(jnp.bfloat16)
    row_count = lax.axis_size("expert") * latent_kv.shape[0]
    nope_flat = dkey_low[:, :, :NOPE].reshape(row_count, heads_here * NOPE)
    lat_term = lax.dot_general(
        nope_flat, w_uk, CONTRACT_LAST, preferred_element_type=jnp.float32
    ) + lax.dot_general(
        dval_low.reshape(row_count, heads_here * VD),
        w_uv,
        CONTRACT_LAST,
        preferred_element_type=jnp.float32,
    )
    rope_term = jnp.sum(dkey_low[:, :, NOPE:].astype(jnp.float32), axis=1)
    own_rows = lax.psum_scatter(
        jnp.concatenate([lat_term, rope_term], axis=1), "expert", scatter_dimension=0, tiled=True
    )
    d_latent = lax.psum_scatter(own_rows, "head", scatter_dimension=1, tiled=True)
    return (d_query, d_latent.astype(jnp.bfloat16))


def body(
    hidden_in,
    grad_out,
    expert_ids,
    gate_weights,
    w_gate,
    w_up,
    w_down,
    latent_kv,
    query,
    d_attn,
    w_uk,
    w_uv,
    doc_ids,
):
    d_query, d_latent_kv = attention_half(latent_kv, query, d_attn, w_uk, w_uv, doc_ids)
    d_hidden, d_gates = expert_half(
        hidden_in, grad_out, expert_ids, gate_weights, w_gate, w_up, w_down
    )
    return (d_hidden, d_gates, d_query, d_latent_kv)


def solution(mesh):
    placed = (
        P(("dp", "expert"), "head"),
        P(("dp", "expert"), "head"),
        P(("dp", "expert"), None),
        P(("dp", "expert"), None),
        P(("dp", "expert"), None, "head"),
        P(("dp", "expert"), None, "head"),
        P(("dp", "expert"), "head", None),
        P(("dp", "expert"), None),
        P("dp", ("expert", "head")),
        P("dp", ("expert", "head")),
        P(None, ("expert", "head")),
        P(None, ("expert", "head")),
        P("dp"),
    )
    return jax.shard_map(
        body,
        mesh=mesh,
        in_specs=placed,
        out_specs=(
            P(("dp", "expert"), "head"),
            P(("dp", "expert"), None),
            P("dp", ("expert", "head")),
            P(("dp", "expert"), "head"),
        ),
        check_vma=False,
    )
```

profile of v0, /device:TPU:0, one launch (start us, length us, event | category | flops | bytes accessed | tf_op | source)
XLA Modules:
  0.0 199.1 jit_solution(16776576463837883362)
XLA Ops:
  8.3 2.3 %reduce-window.6 = s32[8,8,128]{2,1,0:T(8,128)S(1)} reduce-window(s32[8,8,128]{2,1,0:T(8,128)S(1)} %fusion.39, s32[]{:T(128)} %constant.44.clone.1), window={size=1x1x128 pad=0_0x0_0x127_0}, to_apply=%region_0.1 | reduce-window | flops 1040384 | bytes 65540 | tf_op jit(solution)/shard_map/reduce-window
  13.8 7.3 %all-to-all-start.1 = ((bf16[8,8,1792]{2,1,0:T(8,128)(2,1)}), bf16[8,8,1792]{2,1,0:T(8,128)(2,1)S(1)}, u32[]{:S(2)}, u32[]{:S(2)}) async-start(bf16[8,8,1792]{2,1,0:T(8,128)(2,1)} %get-tuple-element.34), calls=%async_computation.1 | async-start | bytes 458752 | tf_op jit(solution)/shard_map/all_to_all | solution.py:59
  21.3 7.8 %all_gather.11 = bf16[256,576]{0,1:T(8,128)(2,1)S(1)} all-gather(bf16[128,576]{0,1:T(8,128)(2,1)S(1)} %copy-done.5), channel_id=1, replica_groups=mesh['dp'=4,'expert'=2,'head'=4] {'expert'}, dimensions={0}, use_global_device_ids=true | all-gather | bytes 442368 | tf_op jit(solution)/shard_map/all_gather | solution.py:94
  30.5 2.0 fusion.11
  37.4 3.6 %fusion.60 = (f32[8,256]{1,0:T(8,128)S(1)}, f32[8,256,256]{1,2,0:T(8,128)}) fusion(pred[256,256]{0,1:T(8,128)(4,1)S(1)} %fusion.31, bf16[256,8,192]{0,2,1:T(8,128)(2,1)} %bitcast.185, bf16[256,8,64]{0,2,1:T(8,128)(2,1)} %broadcast_in_dim.128, bf16[256,8,128]{0,2,1:T(8,128)(2,1)} %bitcast.188), kind=kOutput, calls=%fused_computation.174 | convolution fusion | flops 204996864 | bytes 3743744 | tf_op jit(solution)/shard_map/sub | solution.py:127
  41.0 2.9 %convolution_convert_fusion.3 = bf16[8,256,128]{1,2,0:T(8,128)(2,1)} fusion(bf16[256,8,128]{0,2,1:T(8,128)(2,1)S(1)} %bitcast.180, f32[8,256,256]{1,2,0:T(8,128)} %get-tuple-element.102, f32[8,256]{1,0:T(8,128)S(1)} %get-tuple-element.101), kind=kOutput, calls=%fused_computation.32 | convolution fusion | flops 135528448 | bytes 3153920 | tf_op jit(solution)/shard_map/hqk,qhd->khd/dot_general | solution.py:143
  43.9 4.2 %fusion.19 = bf16[256,8,192]{0,2,1:T(8,128)(2,1)} fusion(bf16[256,8,192]{0,2,1:T(8,128)(2,1)} %bitcast.186, f32[8,256,256]{2,1,0:T(8,128)S(1)} %fusion.61, f32[8,256,256]{1,2,0:T(8,128)} %get-tuple-element.102, f32[8,256]{1,0:T(8,128)S(1)} %get-tuple-element.101), kind=kOutput, calls=%fused_computation.33 | convolution fusion | flops 205392128 | bytes 5775360 | tf_op jit(solution)/shard_map/hqk,qhd->khd/dot_general | solution.py:140
  53.4 1.9 convolution_add_fusion.1
  56.2 4.8 %all-to-all-start = ((bf16[8,8,1792]{2,1,0:T(8,128)(2,1)}), bf16[8,8,1792]{2,1,0:T(8,128)(2,1)S(1)}, u32[]{:S(2)}, u32[]{:S(2)}) async-start(bf16[8,8,1792]{2,1,0:T(8,128)(2,1)} %get-tuple-element.33), calls=%async_computation | async-start | bytes 458752 | tf_op jit(solution)/shard_map/all_to_all | solution.py:60
  61.1 9.5 %all_gather.10 = bf16[8,8,7168]{2,1,0:T(8,128)(2,1)S(1)} all-gather(bf16[8,8,1792]{2,1,0:T(8,128)(2,1)S(1)} %all-to-all-done.1), channel_id=1, replica_groups=mesh['dp'=4,'expert'=2,'head'=4] {'head'}, dimensions={2}, use_global_device_ids=true | all-gather | bytes 1146880 | tf_op jit(solution)/shard_map/all_gather | solution.py:62
  70.5 4.6 %fusion.4 = f32[64,512]{1,0:T(8,128)S(1)} fusion(bf16[1,7168,512]{2,1,0:T(8,128)(2,1)} %param.19, bf16[8,8,7168]{2,1,0:T(8,128)(2,1)S(1)} %all_gather.10), kind=kOutput, calls=%fused_computation.8 | convolution fusion | flops 469762048 | bytes 8388608 | tf_op jit(solution)/shard_map/dot_general | solution.py:17
  76.6 9.6 %all_gather.9 = bf16[8,8,7168]{2,1,0:T(8,128)(2,1)S(1)} all-gather(bf16[8,8,1792]{2,1,0:T(8,128)(2,1)S(1)} %all-to-all-done), channel_id=1, replica_groups=mesh['dp'=4,'expert'=2,'head'=4] {'head'}, dimensions={2}, use_global_device_ids=true | all-gather | bytes 1146880 | tf_op jit(solution)/shard_map/all_gather | solution.py:63
  86.2 5.7 %multiply_reduce_fusion.1 = (f32[64]{0:T(128)S(1)}, f32[64,512]{1,0:T(8,128)S(1)}) fusion(f32[64,512]{1,0:T(8,128)S(1)} %fusion.7, f32[64,512]{1,0:T(8,128)S(1)} %fusion.4, bf16[1,512,7168]{2,1,0:T(8,128)(2,1)} %param.21, bf16[8,8,7168]{2,1,0:T(8,128)(2,1)S(1)} %all_gather.9), kind=kOutput, calls=%fused_computation.60 | convolution fusion | flops 469991360 | bytes 8651008 | tf_op jit(solution)/shard_map/dot_general | solution.py:19
  91.9 5.5 %fusion.2 = f32[64,7168]{1,0:T(8,128)S(1)} fusion(bf16[1,7168,512]{2,1,0:T(8,128)(2,1)} %param.19, f32[64,512]{1,0:T(8,128)S(1)} %fusion.4, f32[64,512]{1,0:T(8,128)S(1)} %get-tuple-element.100, f32[64,512]{1,0:T(8,128)S(1)} %fusion.7), kind=kOutput, calls=%fused_computation.6 | convolution fusion | flops 470089728 | bytes 9568256 | tf_op jit(solution)/shard_map/dot_general | solution.py:29
  97.5 3.6 %convolution_add_fusion = f32[64,7168]{1,0:T(8,128)} fusion(f32[64,7168]{1,0:T(8,128)S(1)} %fusion.2, bf16[1,7168,512]{2,1,0:T(8,128)(2,1)S(1)} %bitcast.178, f32[64,512]{1,0:T(8,128)S(1)} %get-tuple-element.100, f32[64,512]{1,0:T(8,128)S(1)} %fusion.4), kind=kOutput, calls=%fused_computation.5 | convolution fusion | flops 470417408 | bytes 11272192 | tf_op jit(solution)/shard_map/dot_general | solution.py:31
  102.3 3.3 %convolution_convert_fusion.2 = bf16[8,192,256]{2,1,0:T(8,128)(2,1)S(1)} fusion(f32[8,256,256]{2,1,0:T(8,128)S(1)} %fusion.61, bf16[256,8,64]{0,2,1:T(8,128)(2,1)} %broadcast_in_dim.128, bf16[256,8,128]{0,2,1:T(8,128)(2,1)} %bitcast.189, f32[8,256,256]{1,2,0:T(8,128)} %get-tuple-element.102, f32[8,256]{1,0:T(8,128)S(1)} %get-tuple-element.101), kind=kOutput, calls=%fused_computation.31 | convolution fusion | flops 206964992 | bytes 5775360 | tf_op jit(solution)/shard_map/hqk,khd->qhd/dot_general | solution.py:136
  105.7 6.4 %all-reduce = bf16[64,4]{0,1:T(4,128)(2,1)S(1)} all-reduce(f32[64,4]{0,1:T(4,128)S(1)} %broadcast_in_dim.125), channel_id=3, replica_groups=mesh['dp'=4,'expert'=2,'head'=4] {'head'}, use_global_device_ids=true, to_apply=%region_8.10.clone | all-reduce | flops 256 | bytes 1536
  113.5 5.7 %all-to-all-start.3 = ((bf16[8,1,8]{2,1,0:T(2,128)(2,1)}), bf16[8,1,8]{2,1,0:T(2,128)(2,1)S(1)}, u32[]{:S(2)}, u32[]{:S(2)}) async-start(bf16[8,1,8]{2,1,0:T(2,128)(2,1)} %convert_element_type.97), calls=%async_computation.4 | async-start | bytes 8192 | tf_op jit(solution)/shard_map/all_to_all | solution.py:77
  120.4 5.1 %all-to-all-done.3 = bf16[8,1,8]{2,1,0:T(2,128)(2,1)S(1)} async-done(((bf16[8,1,8]{2,1,0:T(2,128)(2,1)}), bf16[8,1,8]{2,1,0:T(2,128)(2,1)S(1)}, u32[]{:S(2)}, u32[]{:S(2)}) %all-to-all-start.3) | async-done | bytes 160 | tf_op jit(solution)/shard_map/all_to_all | solution.py:77
  128.5 1.8 copy.104
  133.3 5.5 %all-to-all-start.2 = ((bf16[8,8,1792]{2,1,0:T(8,128)(2,1)}), bf16[8,8,1792]{2,1,0:T(8,128)(2,1)S(1)}, u32[]{:S(2)}, u32[]{:S(2)}) async-start(bf16[8,8,1792]{2,1,0:T(8,128)(2,1)} %convert_bitcast_fusion), calls=%async_computation.3 | async-start | bytes 458752 | tf_op jit(solution)/shard_map/all_to_all | solution.py:76
  138.8 39.9 %compare_select_fusion.2 = bf16[1024]{0:T(1024)(128)(2,1)S(1)} fusion(s32[1024]{0:T(1024)S(1)} %bitcast.193, bf16[]{:T(256)} %bitcast.13, bf16[]{:T(256)} %bitcast.14, bf16[]{:T(256)} %bitcast.15, bf16[]{:T(256)} %bitcast.16, bf16[]{:T(256)} %bitcast.17, bf16[]{:T(256)} %bitcast.18, bf16[]{:T(256)} %bitcast.19, bf16[]{:T(256)} %bitcast.20, bf16[]{:T(256)} %bitcast.21, ...), kind=kLoop, calls=%fused_computation.85 | loop fusion | flops 129024 | bytes 6272 | tf_op jit(solution)/shard_map/jit(_take)/gather | solution.py:85
  181.2 5.8 %gather_fusion = bf16[1024,1792]{1,0:T(8,128)(2,1)} fusion(bf16[64,1792]{1,0:T(8,128)(2,1)S(1)} %bitcast.174, s32[1024]{0:T(1024)S(1)} %broadcast_clamp_fusion), kind=kCustom, calls=%fused_computation.2 | custom fusion | bytes 7344128 | tf_op jit(solution)/shard_map/jit(_take)/gather | solution.py:83
  187.0 5.6 %multiply_reduce_fusion = bf16[128,1792]{1,0:T(8,128)(2,1)} fusion(bf16[1024,1792]{1,0:T(8,128)(2,1)} %gather_fusion, f32[128,8]{1,0:T(8,128)S(1)} %get-tuple-element.27, pred[128,8]{1,0:T(8,128)(4,1)S(1)} %get-tuple-element.26), kind=kLoop, calls=%fused_computation.15 | loop fusion | flops 7110656 | bytes 4133888 | tf_op jit(solution)/shard_map/reduce_sum | solution.py:84
  (95 shorter events, 30.6 us)
Async XLA Ops:
  7.2 4.2 %copy-start = (bf16[128,1792]{1,0:T(8,128)(2,1)S(1)}, bf16[128,1792]{1,0:T(8,128)(2,1)}, u32[]{:S(2)}) copy-start(bf16[128,1792]{1,0:T(8,128)(2,1)} %param.15) | copy-start | bytes 1376260
  7.2 5.0 %copy-start.1 = (bf16[128,1792]{1,0:T(8,128)(2,1)S(1)}, bf16[128,1792]{1,0:T(8,128)(2,1)}, u32[]{:S(2)}) copy-start(bf16[128,1792]{1,0:T(8,128)(2,1)} %param.16) | copy-start | bytes 1376260
  12.2 9.0 %copy-start.7 = (s32[256]{0:T(256)S(1)}, s32[256]{0:T(256)}, u32[]{:S(2)}) copy-start(s32[256]{0:T(256)} %param.27) | copy-start | bytes 3076
  12.2 9.1 %copy-start.5 = (bf16[128,576]{0,1:T(8,128)(2,1)S(1)}, bf16[128,576]{0,1:T(8,128)(2,1)}, u32[]{:S(2)}) copy-start(bf16[128,576]{0,1:T(8,128)(2,1)} %param.22) | copy-start | bytes 442372
  12.2 18.3 %copy-start.2 = (bf16[512,1024]{1,0:T(8,128)(2,1)S(1)}, bf16[512,1024]{1,0:T(8,128)(2,1)}, u32[]{:S(2)}) copy-start(bf16[512,1024]{1,0:T(8,128)(2,1)} %param.25) | copy-start | bytes 3145732
  13.8 42.4 %all-to-all-start.1 = ((bf16[8,8,1792]{2,1,0:T(8,128)(2,1)}), bf16[8,8,1792]{2,1,0:T(8,128)(2,1)S(1)}, u32[]{:S(2)}, u32[]{:S(2)}) async-start(bf16[8,8,1792]{2,1,0:T(8,128)(2,1)} %get-tuple-element.34), calls=%async_computation.1 | async-start | bytes 458752 | tf_op jit(solution)/shard_map/all_to_all | solution.py:59
  21.1 107.4 %reduce-scatter.8.cloned.1.call-start = ((), (), s32[]{:S(2)}) async-start(), calls=%async_computation.8 | async-start | bytes 983040 | tf_op jit(solution)/shard_map/reduce_scatter | solution.py:160
  29.1 1.4 copy-start.4
  32.5 1.5 copy-start.3
  34.0 2.7 %slice-start.4 = ((bf16[256,576]{0,1:T(8,128)(2,1)}), bf16[256,64]{0,1:T(8,128)(2,1)S(1)}, s32[]{:S(2)}) async-start(bf16[256,576]{0,1:T(8,128)(2,1)} %copy-done.4), calls=%async_computation.14 | async-start | bytes 65536 | tf_op jit(solution)/shard_map/slice | solution.py:98
  56.2 20.4 %all-to-all-start = ((bf16[8,8,1792]{2,1,0:T(8,128)(2,1)}), bf16[8,8,1792]{2,1,0:T(8,128)(2,1)S(1)}, u32[]{:S(2)}, u32[]{:S(2)}) async-start(bf16[8,8,1792]{2,1,0:T(8,128)(2,1)} %get-tuple-element.33), calls=%async_computation | async-start | bytes 458752 | tf_op jit(solution)/shard_map/all_to_all | solution.py:60
  61.0 70.5 %reduce-scatter.6.cloned.1.call-start = ((), (), s32[]{:S(2)}) async-start(), calls=%async_computation.7 | async-start | bytes 2293760 | tf_op jit(solution)/shard_map/reduce_scatter | solution.py:71
  61.1 14.1 %slice-start = ((s8[7340032]{0:T(1024)(128)(4,1)}), s8[4194304]{0:T(1024)(128)(4,1)S(1)}, s32[]{:S(2)}) async-start(s8[7340032]{0:T(1024)(128)(4,1)} %bitcast.175), calls=%async_computation.10 | async-start | bytes 8388608
  70.5 4.7 %slice-start.1 = ((s8[7340032]{0:T(1024)(128)(4,1)}), s8[3145728]{0:T(1024)(128)(4,1)S(1)}, s32[]{:S(2)}) async-start(s8[7340032]{0:T(1024)(128)(4,1)} %bitcast.175), calls=%async_computation.11 | async-start | bytes 6291456
  86.2 11.3 %slice-start.2 = ((s8[7340032]{0:T(1024)(128)(4,1)}), s8[4194304]{0:T(1024)(128)(4,1)S(1)}, s32[]{:S(2)}) async-start(s8[7340032]{0:T(1024)(128)(4,1)} %bitcast.177), calls=%async_computation.12 | async-start | bytes 8388608
  91.9 5.6 %slice-start.3 = ((s8[7340032]{0:T(1024)(128)(4,1)}), s8[3145728]{0:T(1024)(128)(4,1)S(1)}, s32[]{:S(2)}) async-start(s8[7340032]{0:T(1024)(128)(4,1)} %bitcast.177), calls=%async_computation.13 | async-start | bytes 6291456
  97.5 3.7 %copy-start.6 = (f32[128,8]{0,1:T(8,128)S(1)}, f32[128,8]{0,1:T(8,128)}, u32[]{:S(2)}) copy-start(f32[128,8]{0,1:T(8,128)} %param.18) | copy-start | bytes 12292
  101.1 0.7 copy-start.8
  113.5 12.1 %all-to-all-start.3 = ((bf16[8,1,8]{2,1,0:T(2,128)(2,1)}), bf16[8,1,8]{2,1,0:T(2,128)(2,1)S(1)}, u32[]{:S(2)}, u32[]{:S(2)}) async-start(bf16[8,1,8]{2,1,0:T(2,128)(2,1)} %convert_element_type.97), calls=%async_computation.4 | async-start | bytes 8192 | tf_op jit(solution)/shard_map/all_to_all | solution.py:77
  119.1 60.3 %reduce-scatter.10.cloned.1.call-start = ((), (), s32[]{:S(2)}) async-start(), calls=%async_computation.9 | async-start | bytes 368640
  133.3 47.9 %all-to-all-start.2 = ((bf16[8,8,1792]{2,1,0:T(8,128)(2,1)}), bf16[8,8,1792]{2,1,0:T(8,128)(2,1)S(1)}, u32[]{:S(2)}, u32[]{:S(2)}) async-start(bf16[8,8,1792]{2,1,0:T(8,128)(2,1)} %convert_bitcast_fusion), calls=%async_computation.3 | async-start | bytes 458752 | tf_op jit(solution)/shard_map/all_to_all | solution.py:76
Sparse Core Ops, SparseCore 0:
  56.3 18.3 reduce-scatter.7
  101.2 30.2 reduce-scatter.5
  134.6 20.2 reduce-scatter.9
where the time goes:
time: 201 us; the launch traced here: 199 us
  other arithmetic  53.6 us (27%)
  matrix products  41.9 us (21%)
  blocking collectives  33.3 us (17%)
  local copies, waits for them, and re-layouts  26.4 us (13%)
  starting transfers between devices  23.3 us (12%)
  between operations  14.2 us (7%)
  waiting for transfers between devices  6.3 us (3%)
    gather x1, other arithmetic, expert_half(): jnp.take(flat_gate, safe_target)  39.9 us
    all_gather x1, blocking collectives, expert_half(): lax.all_gather(got_dy, 'head', axis=2, tiled=True)  9.6 us
    all_gather x1, blocking collectives, expert_half(): lax.all_gather(got_x, 'head', axis=2, tiled=True)  9.47 us
    unnamed x35, local copies, waits for them, and re-layouts  8.81 us
    all_gather x1, blocking collectives, attention_half(): piece = lax.all_gather(latent_kv, 'expert', axis=0, tiled=True)  7.85 us
    all_to_all x1, starting transfers between devices, expert_half(): lax.all_to_all(send_x, ('dp', 'expert'), split_axis=0, concat_axis=0, til...  7.25 us
    unnamed x1, blocking collectives  6.42 us
    gather x1, local copies, waits for them, and re-layouts, expert_half(): jnp.take(flat_back, safe_target, axis=0).astype(jnp.float32)  5.82 us
  transfers between devices with their start and end apart: 7, of which 2 were waited for; matrix products, arithmetic and copies ran while one was open for 52% of the time, Pallas kernels for 0%

commit v1 on v0

--- a/solution.py
+++ b/solution.py
@@ -11,6 +11,22 @@
 VD = 128
 CAP = 8
 CONTRACT_LAST = (((1,), (1,)), ((), ()))
+
+
+def exchange_in_pairs(value, axis, split, join):
+    ways, here = (lax.axis_size(axis), lax.axis_index(axis))
+    width = value.shape[split] // ways
+    shape = list(value.shape)
+    shape[split] = width
+    height = shape[join]
+    shape[join] = height * ways
+    full = jnp.zeros(shape, value.dtype)
+    for mask in range(ways):
+        part = lax.dynamic_slice_in_dim(value, (here ^ mask) * width, width, axis=split)
+        if mask:
+            part = lax.ppermute(part, axis, [(d, d ^ mask) for d in range(ways)])
+        full = lax.dynamic_update_slice_in_dim(full, part, (here ^ mask) * height, axis=join)
+    return full
 
 
 def expert_backward(rows_x, rows_dy, gate_mat, up_mat, down_mat):
@@ -73,7 +89,7 @@
     back_rows = summed.astype(jnp.bfloat16).reshape(sources, items, summed.shape[1])
     back_gate = gate_sum[:, 0].astype(jnp.bfloat16).reshape(sources, items)
     back_rows, back_gate = (
-        lax.all_to_all(back_rows, ("dp", "expert"), split_axis=0, concat_axis=0, tiled=True),
+        exchange_in_pairs(back_rows, ("dp", "expert"), 0, 0),
         lax.all_to_all(back_gate, ("dp", "expert"), split_axis=0, concat_axis=0, tiled=True),
     )
     flat_back = back_rows.reshape(window_size * CAP, back_rows.shape[2])

time: 201 us -> 230 us (1.14)
  waiting for transfers between devices: 6.3 us -> 27.5 us
  starting transfers between devices: 23.3 us -> 28.9 us
  local copies, waits for them, and re-layouts: 26.4 us -> 28.7 us
    unnamed x4, waiting for transfers between devices: 0.05 us -> 15.3 us
    ppermute x0 -> x7, starting transfers between devices: none -> 11.1 us  [exchange_in_pairs(): part = lax.ppermute(part, axis, [(d, d ^ mask) for d in range(ways)])]
    ppermute x0 -> x7, waiting for transfers between devices: none -> 5.82 us  [exchange_in_pairs(): part = lax.ppermute(part, axis, [(d, d ^ mask) for d in range(ways)])]
    all_to_all x1 -> x0, starting transfers between devices: 5.51 us -> none  [expert_half(): lax.all_to_all(back_rows, ('dp', 'expert'), split_axis=0, concat_axis=0,...]
    unnamed x35 -> x37, local copies, waits for them, and re-layouts: 8.81 us -> 9.18 us
  transfers between devices with their start and end apart: 7 -> 13, of which waited for: 2 -> 4; matrix products, arithmetic and copies ran while one was open for 52% -> 46% of each run, Pallas kernels for 0% -> 0%
where the time goes in v1:
time: 230 us; the launch traced here: 229 us
  other arithmetic  53.6 us (23%)
  matrix products  42.4 us (18%)
  blocking collectives  33.3 us (14%)
  starting transfers between devices  28.9 us (13%)
  local copies, waits for them, and re-layouts  28.7 us (12%)
  waiting for transfers between devices  27.5 us (12%)
  between operations  14.3 us (6%)
    gather x1, other arithmetic, expert_half(): jnp.take(flat_gate, safe_target)  39.9 us
    unnamed x4, waiting for transfers between devices  15.3 us
    ppermute x7, starting transfers between devices, exchange_in_pairs(): part = lax.ppermute(part, axis, [(d, d ^ mask) for d in range(ways)])  11.1 us
    all_gather x1, blocking collectives, expert_half(): lax.all_gather(got_dy, 'head', axis=2, tiled=True)  9.6 us
    all_gather x1, blocking collectives, expert_half(): lax.all_gather(got_x, 'head', axis=2, tiled=True)  9.47 us
    unnamed x37, local copies, waits for them, and re-layouts  9.18 us
    all_gather x1, blocking collectives, attention_half(): piece = lax.all_gather(latent_kv, 'expert', axis=0, tiled=True)  7.85 us
    all_to_all x1, starting transfers between devices, expert_half(): lax.all_to_all(send_x, ('dp', 'expert'), split_axis=0, concat_axis=0, til...  7.25 us
  transfers between devices with their start and end apart: 13, of which 4 were waited for; matrix products, arithmetic and copies ran while one was open for 46% of the time, Pallas kernels for 0%

profile of v1, /device:TPU:0, one launch (start us, length us, event | category | flops | bytes accessed | tf_op | source)
XLA Modules:
  0.0 228.9 jit_solution(17733415304714959465)
XLA Ops:
  13.8 7.3 %all-to-all-start.1 = ((bf16[8,8,1792]{2,1,0:T(8,128)(2,1)}), bf16[8,8,1792]{2,1,0:T(8,128)(2,1)S(1)}, u32[]{:S(2)}, u32[]{:S(2)}) async-start(bf16[8,8,1792]{2,1,0:T(8,128)(2,1)} %get-tuple-element.42), calls=%async_computation.1 | async-start | bytes 458752 | tf_op jit(solution)/shard_map/all_to_all | solution.py:75
  21.3 7.8 %all_gather.11 = bf16[256,576]{0,1:T(8,128)(2,1)S(1)} all-gather(bf16[128,576]{0,1:T(8,128)(2,1)S(1)} %copy-done.5), channel_id=1, replica_groups=mesh['dp'=4,'expert'=2,'head'=4] {'expert'}, dimensions={0}, use_global_device_ids=true | all-gather | bytes 442368 | tf_op jit(solution)/shard_map/all_gather | solution.py:110
  37.4 3.6 %fusion.60 = (f32[8,256]{1,0:T(8,128)S(1)}, f32[8,256,256]{1,2,0:T(8,128)}) fusion(pred[256,256]{0,1:T(8,128)(4,1)S(1)} %fusion.31, bf16[256,8,192]{0,2,1:T(8,128)(2,1)} %bitcast.184, bf16[256,8,64]{0,2,1:T(8,128)(2,1)} %broadcast_in_dim.132, bf16[256,8,128]{0,2,1:T(8,128)(2,1)} %bitcast.188), kind=kOutput, calls=%fused_computation.189 | convolution fusion | flops 204996864 | bytes 3743744 | tf_op jit(solution)/shard_map/sub | solution.py:143
  41.0 2.9 %convolution_convert_fusion.3 = bf16[8,256,128]{1,2,0:T(8,128)(2,1)} fusion(bf16[256,8,128]{0,2,1:T(8,128)(2,1)S(1)} %bitcast.180, f32[8,256,256]{1,2,0:T(8,128)} %get-tuple-element.110, f32[8,256]{1,0:T(8,128)S(1)} %get-tuple-element.109), kind=kOutput, calls=%fused_computation.32 | convolution fusion | flops 135528448 | bytes 3153920 | tf_op jit(solution)/shard_map/hqk,qhd->khd/dot_general | solution.py:159
  43.9 4.2 %fusion.19 = bf16[256,8,192]{0,2,1:T(8,128)(2,1)} fusion(bf16[256,8,192]{0,2,1:T(8,128)(2,1)} %bitcast.185, f32[8,256,256]{2,1,0:T(8,128)S(1)} %fusion.61, f32[8,256,256]{1,2,0:T(8,128)} %get-tuple-element.110, f32[8,256]{1,0:T(8,128)S(1)} %get-tuple-element.109), kind=kOutput, calls=%fused_computation.33 | convolution fusion | flops 205392128 | bytes 5775360 | tf_op jit(solution)/shard_map/hqk,qhd->khd/dot_general | solution.py:156
  56.2 4.8 %all-to-all-start = ((bf16[8,8,1792]{2,1,0:T(8,128)(2,1)}), bf16[8,8,1792]{2,1,0:T(8,128)(2,1)S(1)}, u32[]{:S(2)}, u32[]{:S(2)}) async-start(bf16[8,8,1792]{2,1,0:T(8,128)(2,1)} %get-tuple-element.41), calls=%async_computation | async-start | bytes 458752 | tf_op jit(solution)/shard_map/all_to_all | solution.py:76
  61.1 9.5 %all_gather.10 = bf16[8,8,7168]{2,1,0:T(8,128)(2,1)S(1)} all-gather(bf16[8,8,1792]{2,1,0:T(8,128)(2,1)S(1)} %all-to-all-done.1), channel_id=1, replica_groups=mesh['dp'=4,'expert'=2,'head'=4] {'head'}, dimensions={2}, use_global_device_ids=true | all-gather | bytes 1146880 | tf_op jit(solution)/shard_map/all_gather | solution.py:78
  70.6 4.7 %fusion.4 = f32[64,512]{1,0:T(8,128)S(1)} fusion(bf16[1,7168,512]{2,1,0:T(8,128)(2,1)} %param.19, bf16[8,8,7168]{2,1,0:T(8,128)(2,1)S(1)} %all_gather.10), kind=kOutput, calls=%fused_computation.8 | convolution fusion | flops 469762048 | bytes 8388608 | tf_op jit(solution)/shard_map/dot_general | solution.py:33
  76.6 9.6 %all_gather.9 = bf16[8,8,7168]{2,1,0:T(8,128)(2,1)S(1)} all-gather(bf16[8,8,1792]{2,1,0:T(8,128)(2,1)S(1)} %all-to-all-done), channel_id=1, replica_groups=mesh['dp'=4,'expert'=2,'head'=4] {'head'}, dimensions={2}, use_global_device_ids=true | all-gather | bytes 1146880 | tf_op jit(solution)/shard_map/all_gather | solution.py:79
  86.2 6.2 %multiply_reduce_fusion.1 = (f32[64]{0:T(128)}, f32[64,512]{1,0:T(8,128)S(1)}) fusion(f32[64,512]{1,0:T(8,128)S(1)} %fusion.7, f32[64,512]{1,0:T(8,128)S(1)} %fusion.4, bf16[1,512,7168]{2,1,0:T(8,128)(2,1)} %param.21, bf16[8,8,7168]{2,1,0:T(8,128)(2,1)S(1)} %all_gather.9), kind=kOutput, calls=%fused_computation.60 | convolution fusion | flops 469991360 | bytes 8651008 | tf_op jit(solution)/shard_map/dot_general | solution.py:35
  92.5 5.5 %fusion.2 = f32[64,7168]{1,0:T(8,128)S(1)} fusion(bf16[1,7168,512]{2,1,0:T(8,128)(2,1)} %param.19, f32[64,512]{1,0:T(8,128)S(1)} %fusion.4, f32[64,512]{1,0:T(8,128)S(1)} %get-tuple-element.108, f32[64,512]{1,0:T(8,128)S(1)} %fusion.7), kind=kOutput, calls=%fused_computation.6 | convolution fusion | flops 470089728 | bytes 9568256 | tf_op jit(solution)/shard_map/dot_general | solution.py:45
  98.0 3.6 %convolution_add_fusion = f32[64,7168]{1,0:T(8,128)} fusion(f32[64,7168]{1,0:T(8,128)S(1)} %fusion.2, bf16[1,7168,512]{2,1,0:T(8,128)(2,1)S(1)} %bitcast.178, f32[64,512]{1,0:T(8,128)S(1)} %get-tuple-element.108, f32[64,512]{1,0:T(8,128)S(1)} %fusion.4), kind=kOutput, calls=%fused_computation.5 | convolution fusion | flops 470417408 | bytes 11272192 | tf_op jit(solution)/shard_map/dot_general | solution.py:47
  103.3 3.3 %convolution_convert_fusion.2 = bf16[8,192,256]{2,1,0:T(8,128)(2,1)S(1)} fusion(f32[8,256,256]{2,1,0:T(8,128)S(1)} %fusion.61, bf16[256,8,64]{0,2,1:T(8,128)(2,1)} %broadcast_in_dim.132, bf16[256,8,128]{0,2,1:T(8,128)(2,1)} %bitcast.189, f32[8,256,256]{1,2,0:T(8,128)} %get-tuple-element.110, f32[8,256]{1,0:T(8,128)} %copy-done.9), kind=kOutput, calls=%fused_computation.31 | convolution fusion | flops 206964992 | bytes 5775360 | tf_op jit(solution)/shard_map/hqk,khd->qhd/dot_general | solution.py:152
  110.4 6.4 %all-reduce = bf16[64,4]{0,1:T(4,128)(2,1)S(1)} all-reduce(f32[64,4]{0,1:T(4,128)S(1)} %broadcast_in_dim.129), channel_id=3, replica_groups=mesh['dp'=4,'expert'=2,'head'=4] {'head'}, use_global_device_ids=true, to_apply=%region_8.10.clone | all-reduce | flops 256 | bytes 1536
  118.2 5.6 %all-to-all-start.2 = ((bf16[8,1,8]{2,1,0:T(2,128)(2,1)}), bf16[8,1,8]{2,1,0:T(2,128)(2,1)S(1)}, u32[]{:S(2)}, u32[]{:S(2)}) async-start(bf16[8,1,8]{2,1,0:T(2,128)(2,1)} %convert_element_type.97), calls=%async_computation.3 | async-start | bytes 8192 | tf_op jit(solution)/shard_map/all_to_all | solution.py:93
  123.9 6.3 %all-to-all-done.2 = bf16[8,1,8]{2,1,0:T(2,128)(2,1)S(1)} async-done(((bf16[8,1,8]{2,1,0:T(2,128)(2,1)}), bf16[8,1,8]{2,1,0:T(2,128)(2,1)S(1)}, u32[]{:S(2)}, u32[]{:S(2)}) %all-to-all-start.2) | async-done | bytes 160 | tf_op jit(solution)/shard_map/all_to_all | solution.py:93
  133.2 39.9 %compare_select_fusion.2 = bf16[1024]{0:T(1024)(128)(2,1)S(1)} fusion(s32[1024]{0:T(1024)S(1)} %bitcast.193, bf16[]{:T(256)} %bitcast.13, bf16[]{:T(256)} %bitcast.14, bf16[]{:T(256)} %bitcast.15, bf16[]{:T(256)} %bitcast.16, bf16[]{:T(256)} %bitcast.17, bf16[]{:T(256)} %bitcast.18, bf16[]{:T(256)} %bitcast.19, bf16[]{:T(256)} %bitcast.20, bf16[]{:T(256)} %bitcast.21, ...), kind=kLoop, calls=%fused_computation.100 | loop fusion | flops 129024 | bytes 6272 | tf_op jit(solution)/shard_map/jit(_take)/gather | solution.py:101
  177.5 15.3 %reduce-scatter.10.cloned.1.call-done = f32[144,128]{1,0:T(8,128)} async-done(((f32[576,128]{1,0:T(8,128)}), f32[144,128]{1,0:T(8,128)}) %reduce-scatter.10.cloned.1.call-update) | async-done | bytes 73744
  194.5 4.2 %collective-permute-start.6 = (bf16[1,8,1792]{2,1,0:T(8,128)(2,1)S(1)}, bf16[1,8,1792]{2,1,0:T(8,128)(2,1)S(1)}, u32[]{:S(2)}, u32[]{:S(2)}) collective-permute-start(bf16[1,8,1792]{2,1,0:T(8,128)(2,1)S(1)} %get-tuple-element.33), channel_id=1, source_target_pairs={{0,28},{4,24},{8,20},{12,16},{16,12},{20,8},{24,4},{28,0},{1,29},{... | collective-permute-start | bytes 86024 | tf_op jit(solution)/shard_map/ppermute | solution.py:27
  199.9 2.3 %collective-permute-start.3 = (bf16[1,8,1792]{2,1,0:T(8,128)(2,1)S(1)}, bf16[1,8,1792]{2,1,0:T(8,128)(2,1)S(1)}, u32[]{:S(2)}, u32[]{:S(2)}) collective-permute-start(bf16[1,8,1792]{2,1,0:T(8,128)(2,1)S(1)} %get-tuple-element.36), channel_id=1, source_target_pairs={{0,16},{4,20},{8,24},{12,28},{16,0},{20,4},{24,8},{28,12},{1,17},{... | collective-permute-start | bytes 86024 | tf_op jit(solution)/shard_map/ppermute | solution.py:27
  203.2 2.9 %collective-permute-done.1 = bf16[1,8,1792]{2,1,0:T(8,128)(2,1)S(1)} collective-permute-done((bf16[1,8,1792]{2,1,0:T(8,128)(2,1)S(1)}, bf16[1,8,1792]{2,1,0:T(8,128)(2,1)S(1)}, u32[]{:S(2)}, u32[]{:S(2)}) %collective-permute-start.1) | collective-permute-done | bytes 28704 | tf_op jit(solution)/shard_map/ppermute | solution.py:27
  207.9 2.9 %collective-permute-done.2 = bf16[1,8,1792]{2,1,0:T(8,128)(2,1)S(1)} collective-permute-done((bf16[1,8,1792]{2,1,0:T(8,128)(2,1)S(1)}, bf16[1,8,1792]{2,1,0:T(8,128)(2,1)S(1)}, u32[]{:S(2)}, u32[]{:S(2)}) %collective-permute-start.2) | collective-permute-done | bytes 28704 | tf_op jit(solution)/shard_map/ppermute | solution.py:27
  210.9 5.8 %gather_fusion = bf16[1024,1792]{1,0:T(8,128)(2,1)} fusion(bf16[64,1792]{1,0:T(8,128)(2,1)S(1)} %bitcast.174, s32[1024]{0:T(1024)S(1)} %broadcast_clamp_fusion), kind=kCustom, calls=%fused_computation.2 | custom fusion | bytes 7344128 | tf_op jit(solution)/shard_map/jit(_take)/gather | solution.py:99
  216.8 5.6 %multiply_reduce_fusion = bf16[128,1792]{1,0:T(8,128)(2,1)} fusion(bf16[1024,1792]{1,0:T(8,128)(2,1)} %gather_fusion, f32[128,8]{1,0:T(8,128)S(1)} %get-tuple-element.27, pred[128,8]{1,0:T(8,128)(4,1)S(1)} %get-tuple-element.26), kind=kLoop, calls=%fused_computation.15 | loop fusion | flops 7110656 | bytes 4133888 | tf_op jit(solution)/shard_map/reduce_sum | solution.py:100
  (118 shorter events, 44.3 us)
Async XLA Ops:
  7.2 4.2 %copy-start = (bf16[128,1792]{1,0:T(8,128)(2,1)S(1)}, bf16[128,1792]{1,0:T(8,128)(2,1)}, u32[]{:S(2)}) copy-start(bf16[128,1792]{1,0:T(8,128)(2,1)} %param.15) | copy-start | bytes 1376260
  7.2 5.0 %copy-start.1 = (bf16[128,1792]{1,0:T(8,128)(2,1)S(1)}, bf16[128,1792]{1,0:T(8,128)(2,1)}, u32[]{:S(2)}) copy-start(bf16[128,1792]{1,0:T(8,128)(2,1)} %param.16) | copy-start | bytes 1376260
  11.1 90.6 %copy-start.6 = (s32[1024]{0:T(1024)}, s32[1024]{0:T(1024)S(1)}, u32[]{:S(2)}) copy-start(s32[1024]{0:T(1024)S(1)} %fusion.38) | copy-start | bytes 12292
  12.2 9.0 %copy-start.8 = (s32[256]{0:T(256)S(1)}, s32[256]{0:T(256)}, u32[]{:S(2)}) copy-start(s32[256]{0:T(256)} %param.27) | copy-start | bytes 3076
  12.2 9.1 %copy-start.5 = (bf16[128,576]{0,1:T(8,128)(2,1)S(1)}, bf16[128,576]{0,1:T(8,128)(2,1)}, u32[]{:S(2)}) copy-start(bf16[128,576]{0,1:T(8,128)(2,1)} %param.22) | copy-start | bytes 442372
  12.2 18.3 %copy-start.2 = (bf16[512,1024]{1,0:T(8,128)(2,1)S(1)}, bf16[512,1024]{1,0:T(8,128)(2,1)}, u32[]{:S(2)}) copy-start(bf16[512,1024]{1,0:T(8,128)(2,1)} %param.25) | copy-start | bytes 3145732
  13.8 42.4 %all-to-all-start.1 = ((bf16[8,8,1792]{2,1,0:T(8,128)(2,1)}), bf16[8,8,1792]{2,1,0:T(8,128)(2,1)S(1)}, u32[]{:S(2)}, u32[]{:S(2)}) async-start(bf16[8,8,1792]{2,1,0:T(8,128)(2,1)} %get-tuple-element.42), calls=%async_computation.1 | async-start | bytes 458752 | tf_op jit(solution)/shard_map/all_to_all | solution.py:75
  21.1 152.1 %reduce-scatter.8.cloned.1.call-start = ((), (), s32[]{:S(2)}) async-start(), calls=%async_computation.7 | async-start | bytes 983040 | tf_op jit(solution)/shard_map/reduce_scatter | solution.py:176
  41.0 2.9 %copy-start.9 = (f32[8,256]{1,0:T(8,128)}, f32[8,256]{1,0:T(8,128)S(1)}, u32[]{:S(2)}) copy-start(f32[8,256]{1,0:T(8,128)S(1)} %get-tuple-element.109) | copy-start | bytes 24580
  56.2 20.4 %all-to-all-start = ((bf16[8,8,1792]{2,1,0:T(8,128)(2,1)}), bf16[8,8,1792]{2,1,0:T(8,128)(2,1)S(1)}, u32[]{:S(2)}, u32[]{:S(2)}) async-start(bf16[8,8,1792]{2,1,0:T(8,128)(2,1)} %get-tuple-element.41), calls=%async_computation | async-start | bytes 458752 | tf_op jit(solution)/shard_map/all_to_all | solution.py:76
  61.0 114.1 %reduce-scatter.6.cloned.1.call-start = ((), (), s32[]{:S(2)}) async-start(), calls=%async_computation.6 | async-start | bytes 2293760 | tf_op jit(solution)/shard_map/reduce_scatter | solution.py:87
  61.1 14.1 %slice-start = ((s8[7340032]{0:T(1024)(128)(4,1)}), s8[4194304]{0:T(1024)(128)(4,1)S(1)}, s32[]{:S(2)}) async-start(s8[7340032]{0:T(1024)(128)(4,1)} %bitcast.175), calls=%async_computation.9 | async-start | bytes 8388608
  70.6 4.7 %slice-start.1 = ((s8[7340032]{0:T(1024)(128)(4,1)}), s8[3145728]{0:T(1024)(128)(4,1)S(1)}, s32[]{:S(2)}) async-start(s8[7340032]{0:T(1024)(128)(4,1)} %bitcast.175), calls=%async_computation.10 | async-start | bytes 6291456
  86.2 11.8 %slice-start.2 = ((s8[7340032]{0:T(1024)(128)(4,1)}), s8[4194304]{0:T(1024)(128)(4,1)S(1)}, s32[]{:S(2)}) async-start(s8[7340032]{0:T(1024)(128)(4,1)} %bitcast.177), calls=%async_computation.11 | async-start | bytes 8388608
  92.5 5.5 %slice-start.3 = ((s8[7340032]{0:T(1024)(128)(4,1)}), s8[3145728]{0:T(1024)(128)(4,1)S(1)}, s32[]{:S(2)}) async-start(s8[7340032]{0:T(1024)(128)(4,1)} %bitcast.177), calls=%async_computation.12 | async-start | bytes 6291456
  118.2 12.0 %all-to-all-start.2 = ((bf16[8,1,8]{2,1,0:T(2,128)(2,1)}), bf16[8,1,8]{2,1,0:T(2,128)(2,1)S(1)}, u32[]{:S(2)}, u32[]{:S(2)}) async-start(bf16[8,1,8]{2,1,0:T(2,128)(2,1)} %convert_element_type.97), calls=%async_computation.3 | async-start | bytes 8192 | tf_op jit(solution)/shard_map/all_to_all | solution.py:93
  123.8 69.0 %reduce-scatter.10.cloned.1.call-start = ((), (), s32[]{:S(2)}) async-start(), calls=%async_computation.8 | async-start | bytes 368640
  176.2 26.0 %collective-permute-start = (bf16[1,8,1792]{2,1,0:T(8,128)(2,1)S(1)}, bf16[1,8,1792]{2,1,0:T(8,128)(2,1)S(1)}, u32[]{:S(2)}, u32[]{:S(2)}) collective-permute-start(bf16[1,8,1792]{2,1,0:T(8,128)(2,1)S(1)} %get-tuple-element.39), channel_id=1, source_target_pairs={{0,4},{4,0},{8,12},{12,8},{16,20},{20,16},{24,28},{28,24},{1,5},{5... | collective-permute-start | bytes 86024 | tf_op jit(solution)/shard_map/ppermute | solution.py:27
  194.5 16.4 %collective-permute-start.6 = (bf16[1,8,1792]{2,1,0:T(8,128)(2,1)S(1)}, bf16[1,8,1792]{2,1,0:T(8,128)(2,1)S(1)}, u32[]{:S(2)}, u32[]{:S(2)}) collective-permute-start(bf16[1,8,1792]{2,1,0:T(8,128)(2,1)S(1)} %get-tuple-element.33), channel_id=1, source_target_pairs={{0,28},{4,24},{8,20},{12,16},{16,12},{20,8},{24,4},{28,0},{1,29},{... | collective-permute-start | bytes 86024 | tf_op jit(solution)/shard_map/ppermute | solution.py:27
  198.8 12.1 %collective-permute-start.5 = (bf16[1,8,1792]{2,1,0:T(8,128)(2,1)S(1)}, bf16[1,8,1792]{2,1,0:T(8,128)(2,1)S(1)}, u32[]{:S(2)}, u32[]{:S(2)}) collective-permute-start(bf16[1,8,1792]{2,1,0:T(8,128)(2,1)S(1)} %get-tuple-element.34), channel_id=1, source_target_pairs={{0,24},{4,28},{8,16},{12,20},{16,8},{20,12},{24,0},{28,4},{1,25},{... | collective-permute-start | bytes 86024 | tf_op jit(solution)/shard_map/ppermute | solution.py:27
  199.2 11.6 %collective-permute-start.4 = (bf16[1,8,1792]{2,1,0:T(8,128)(2,1)S(1)}, bf16[1,8,1792]{2,1,0:T(8,128)(2,1)S(1)}, u32[]{:S(2)}, u32[]{:S(2)}) collective-permute-start(bf16[1,8,1792]{2,1,0:T(8,128)(2,1)S(1)} %get-tuple-element.35), channel_id=1, source_target_pairs={{0,20},{4,16},{8,28},{12,24},{16,4},{20,0},{24,12},{28,8},{1,21},{... | collective-permute-start | bytes 86024 | tf_op jit(solution)/shard_map/ppermute | solution.py:27
  199.9 11.0 %collective-permute-start.3 = (bf16[1,8,1792]{2,1,0:T(8,128)(2,1)S(1)}, bf16[1,8,1792]{2,1,0:T(8,128)(2,1)S(1)}, u32[]{:S(2)}, u32[]{:S(2)}) collective-permute-start(bf16[1,8,1792]{2,1,0:T(8,128)(2,1)S(1)} %get-tuple-element.36), channel_id=1, source_target_pairs={{0,16},{4,20},{8,24},{12,28},{16,0},{20,4},{24,8},{28,12},{1,17},{... | collective-permute-start | bytes 86024 | tf_op jit(solution)/shard_map/ppermute | solution.py:27
  202.2 3.9 %collective-permute-start.1 = (bf16[1,8,1792]{2,1,0:T(8,128)(2,1)S(1)}, bf16[1,8,1792]{2,1,0:T(8,128)(2,1)S(1)}, u32[]{:S(2)}, u32[]{:S(2)}) collective-permute-start(bf16[1,8,1792]{2,1,0:T(8,128)(2,1)S(1)} %get-tuple-element.38), channel_id=1, source_target_pairs={{0,8},{4,12},{8,0},{12,4},{16,24},{20,28},{24,16},{28,20},{1,9},{5... | collective-permute-start | bytes 86024 | tf_op jit(solution)/shard_map/ppermute | solution.py:27
  206.1 4.8 %collective-permute-start.2 = (bf16[1,8,1792]{2,1,0:T(8,128)(2,1)S(1)}, bf16[1,8,1792]{2,1,0:T(8,128)(2,1)S(1)}, u32[]{:S(2)}, u32[]{:S(2)}) collective-permute-start(bf16[1,8,1792]{2,1,0:T(8,128)(2,1)S(1)} %get-tuple-element.37), channel_id=1, source_target_pairs={{0,12},{4,8},{8,4},{12,0},{16,28},{20,24},{24,20},{28,16},{1,13},{... | collective-permute-start | bytes 86024 | tf_op jit(solution)/shard_map/ppermute | solution.py:27
  (4 other events, 6.4 us)
Sparse Core Ops, SparseCore 0:
  56.3 18.3 reduce-scatter.7
  101.7 30.2 reduce-scatter.5
  175.2 17.5 reduce-scatter.9
